TPU v7x, 256 devices: a whole 4x4x8 slice. The times are simulated.
256 devices in a mesh: cls: 2 (over x_lo), row: 128 (over z, x_hi, y, core).
Axes of the slice: x: 4 (x_hi: 2, x_lo: 2; x = x_hi * 2 + x_lo), y: 4, z: 8, core: 2. Of those that a mesh axis runs over, the one named last changes fastest.
Arguments:
- coeffs: bfloat16 [2, 1, 8192, 8192], P('cls', None, 'row'), may hold values from -6 to 6
- h_blocks: bfloat16 [2, 128, 64, 256], P('cls'), may hold values from -0.375 to 0.375
- h_cols: int32 [2, 128, 4], P('cls'), may hold values from 0 to 127, all different within a row
- g_blocks: bfloat16 [2, 128, 64, 128], P('cls'), may hold values from -0.5 to 0.5
- g_cols: int32 [2, 128, 2], P('cls'), may hold values from 0 to 127, all different within a row
Outputs:
- sigma_out: bfloat16 [2, 1, 8192, 8192], P('cls', None, 'row')
Inputs may be any that keep to these rules, and one draw needn't show every extreme that they name: `h_cols`: each block row names 4 different block columns, and every block column is named in at least one of the two classes. `g_cols`: each block row names 2 different block columns, and every block column is named in at least one of the two classes.
All inputs are finite; a program needn't handle non-finite values.
Results may differ from a plain program's by a relative error of at most 0.0043.
Values may be sent and summed in bfloat16 or wider, within the bound.
A program may use at most 128 MiB of HBM per device.

v0:
```python
import functools

import jax
import jax.numpy as jnp
from jax import lax
from jax.experimental import pallas as pl
from jax.experimental.pallas import tpu as pltpu
from jax.sharding import PartitionSpec as P

MESH = pl.DeviceIdType.MESH
NY = 4
BLK = 64
LANES = 128
KH = 4
KG = 2


def hop(k, nz):
    return lax.rem(((k + 1) // 2) * (2 * lax.rem(k, 2) - 1) + nz, nz)


def kernel(nz, ny, c_ref, h_hbm, hc, g_hbm, gc, out_ref, slabs, halves, own, other, prod, back, beta, hv, gv,
           load_sem, s1_send, s1_recv, x_send, x_recv, sib_recv, r_send, r_recv):
    chips = nz * 2 * ny
    plane = 2 * ny
    cls, row = lax.axis_index("cls"), lax.axis_index("row")
    core, p = lax.rem(row, 2), row // 2
    z, xh, y = p // plane, lax.rem(p // ny, 2), lax.rem(p, ny)

    def device(c, z_, xh_, y_, s_):
        return (c, ((z_ * 2 + xh_) * ny + y_) * 2 + s_)

    pair = device(1 - cls, z, xh, y, core)
    side = device(1 - cls, z, 1 - xh, y, core)
    across = device(cls, z, 1 - xh, y, core)
    sibling = device(cls, z, xh, y, 1 - core)

    h_copy = pltpu.make_async_copy(h_hbm.at[0], hv, load_sem.at[0])
    g_copy = pltpu.make_async_copy(g_hbm.at[0], gv, load_sem.at[1])
    h_copy.start()
    g_copy.start()

    barrier = pltpu.get_barrier_semaphore()

    @pl.loop(1, chips)
    def _(i):
        pl.semaphore_signal(barrier, inc=1, device_id=(cls, lax.rem(p + i, chips) * 2 + core), device_id_type=MESH)

    for target in (pair, side, sibling):
        pl.semaphore_signal(barrier, inc=1, device_id=target, device_id_type=MESH)
    pl.semaphore_wait(barrier, chips + 2)

    def remote(src, dst, send, recv, target):
        return pltpu.make_async_remote_copy(
            src_ref=src, dst_ref=dst, send_sem=send, recv_sem=recv, device_id=target, device_id_type=MESH)

    mine = z * ny + y

    @pl.loop(0, nz)
    def _(k):
        to_z = lax.rem(z + hop(k, nz), nz)
        for a in range(2):
            for b in range(ny):
                start = pl.multiple_of(((to_z * 2 + a) * ny + b) * LANES, LANES)
                slabs[to_z * plane + b * 2 + a] = c_ref[0, 0, :, pl.ds(start, LANES)]
        for d in range(ny):
            to_y = lax.rem(y + d, ny)
            src = pl.ds(to_z * plane + to_y * 2, 2)

            def send():
                remote(slabs.at[src], own.at[pl.ds(core * 3 + xh, 2), mine], s1_send.at[k], s1_recv.at[k],
                       device(cls, to_z, xh, to_y, core)).start()

            if d == 0:
                pl.when(k > 0)(send)
            else:
                send()

    own[core * 3 + xh, mine] = slabs[z * plane + y * 2]
    own[core * 3 + xh + 1, mine] = slabs[z * plane + y * 2 + 1]

    low = lax.broadcasted_iota(jnp.int32, (BLK, LANES), 1) < BLK

    @pl.loop(0, chips)
    def _(t):
        wide = c_ref[0, 0, :, pl.ds(pl.multiple_of(t * LANES, LANES), LANES)].astype(jnp.float32)
        turned = pltpu.roll(wide, BLK, 1)
        zero = jnp.zeros_like(wide)
        halves[0, 2 * t] = jnp.where(low, wide, zero).astype(jnp.bfloat16)
        halves[1, 2 * t + 1] = jnp.where(low, zero, wide).astype(jnp.bfloat16)
        halves[0, 2 * t + 1] = jnp.where(low, turned, zero).astype(jnp.bfloat16)
        halves[1, 2 * t] = jnp.where(low, zero, turned).astype(jnp.bfloat16)

    h_copy.wait()

    def beta_slab(q):
        tall = []
        for i in (2 * q, 2 * q + 1):
            wide = [halves[0, hc[0, i, k]] + halves[1, hc[0, i, k + 1]] for k in range(0, KH, 2)]
            tall.append(jnp.concatenate(wide, axis=1))
        blocks = hv[pl.ds(2 * q, 2)].reshape(2 * BLK, KH * BLK)
        both = lax.dot_general(jnp.concatenate(tall, axis=0), blocks, (((1,), (1,)), ((), ())),
                               preferred_element_type=jnp.float32)
        beta[q] = jnp.where(low, both[:BLK], both[BLK:])

    def group(k):
        return pl.ds(lax.rem(z - hop(k, nz) + nz, nz) * ny, ny)

    def forward(k):
        zs = group(k)
        arrived = (other.at[core * 2 + xh, zs], other.at[core * 2 + 1 - xh, zs], own.at[core * 3 + 2 * (1 - xh), zs])
        for n, ref in enumerate(arrived):
            remote(ref, ref, x_send.at[n], x_recv.at[n, k], sibling).wait_recv()
            remote(ref, ref, x_send.at[4 + n], sib_recv.at[1 + n], sibling).start()

    @pl.loop(0, nz)
    def _(k):
        zs = group(k)

        @pl.when(k == 0)
        def _():
            part = own.at[pl.ds(core * 3 + xh, 2), pl.ds(0, ny - 1)]
            remote(part, part, s1_send.at[k], s1_recv.at[k], sibling).wait_recv()

        @pl.when(k > 0)
        def _():
            part = own.at[pl.ds(core * 3 + xh, 2), zs]
            remote(part, part, s1_send.at[k], s1_recv.at[k], sibling).wait_recv()

        straight, transit = own.at[core * 3 + 2 * xh, zs], own.at[core * 3 + 1, zs]
        remote(straight, other.at[core * 2 + xh, zs], x_send.at[0], x_recv.at[0, k], pair).start()
        remote(transit, other.at[core * 2 + xh, zs], x_send.at[1], x_recv.at[1, k], side).start()
        remote(transit, straight, x_send.at[2], x_recv.at[2, k], across).start()
        remote(straight, straight, x_send.at[3], sib_recv.at[0], sibling).start()
        for i in range(plane):
            beta_slab(k * plane + i)

        @pl.when(k > 0)
        def _():
            forward(k - 1)

    forward(nz - 1)
    g_copy.wait()
    theirs = (own.at[(1 - core) * 3 + 2 * xh], other.at[(1 - core) * 2 + xh], other.at[(1 - core) * 2 + 1 - xh],
              own.at[(1 - core) * 3 + 2 * (1 - xh)])
    for n, ref in enumerate(theirs):
        remote(ref, ref, x_send.at[0], sib_recv.at[n], sibling).wait_recv()

    def place(j):
        s, q = lax.rem(j, 2), j // 2
        return s, lax.rem(q // ny, 2), (q // plane) * ny + lax.rem(q, ny)

    def own_rows(j):
        s, a, b = place(j)
        return own[s * 3 + 2 * a, b]

    def other_rows(j):
        s, a, b = place(j)
        return other[s * 2 + a, b]

    def alpha_block(q):
        i = 2 * q + core
        x = jnp.concatenate([own_rows(hc[0, i, k]) for k in range(KH)], axis=0)
        w = jnp.concatenate([other_rows(gc[0, i, k]) for k in range(KG)], axis=0)
        total = jnp.dot(hv[i], x, preferred_element_type=jnp.float32)
        total = total + jnp.dot(gv[i], w, preferred_element_type=jnp.float32)
        prod[q] = total.astype(jnp.bfloat16)

    @pl.loop(0, nz)
    def _(k):
        n = nz - 1 - k
        to_z = lax.rem(z + hop(n, nz), nz)
        for i in range(plane):
            alpha_block(to_z * plane + i)
        for i in range(plane):
            q = to_z * plane + i

            @pl.when(q != p)
            def _():
                remote(prod.at[q], back.at[p], r_send, r_recv.at[n], (cls, 2 * q + core)).start()

            @pl.when(q == p)
            def _():
                back[p] = prod[p]

    @pl.loop(0, nz)
    def _(k):
        n = nz - 1 - k
        from_z = lax.rem(z - hop(n, nz) + nz, nz)

        @pl.when(n == 0)
        def _():
            part = back.at[pl.ds(0, plane - 1)]
            remote(part, part, r_send, r_recv.at[n], sibling).wait_recv()

        @pl.when(n > 0)
        def _():
            part = back.at[pl.ds(from_z * plane, plane)]
            remote(part, part, r_send, r_recv.at[n], sibling).wait_recv()

        for i in range(plane):
            q = from_z * plane + i
            total = beta[q] + back[q].astype(jnp.float32)
            out_ref[0, 0, :, pl.ds(pl.multiple_of(q * LANES, LANES), LANES)] = total.astype(jnp.bfloat16)

    @pl.loop(0, nz)
    def _(k):
        @pl.when(k == 0)
        def _():
            part = slabs.at[pl.ds(0, 2 * (ny - 1))]
            remote(part, part, s1_send.at[k], s1_recv.at[k], sibling).wait_send()

        @pl.when(k > 0)
        def _():
            part = slabs.at[pl.ds(0, plane)]
            remote(part, part, s1_send.at[k], s1_recv.at[k], sibling).wait_send()

    for n in range(7):
        remote(own.at[0], own.at[0], x_send.at[n], sib_recv.at[0], sibling).wait_send()
    part = prod.at[pl.ds(0, chips - 1)]
    remote(part, part, r_send, r_recv.at[0], sibling).wait_send()


def per_device(ny, coeffs, h_blocks, h_cols, g_blocks, g_cols):
    num_blocks = h_cols.shape[1]
    chips = num_blocks // 2
    nz = chips // (2 * ny)
    bf16, dma = jnp.bfloat16, pltpu.SemaphoreType.DMA
    vmem, smem = pl.BlockSpec(memory_space=pltpu.VMEM), pl.BlockSpec(memory_space=pltpu.SMEM)
    hbm = pl.BlockSpec(memory_space=pl.ANY)
    return pl.pallas_call(
        functools.partial(kernel, nz, ny),
        out_shape=jax.ShapeDtypeStruct(coeffs.shape, bf16),
        in_specs=[vmem, hbm, smem, hbm, smem],
        out_specs=vmem,
        scratch_shapes=[
            pltpu.VMEM((chips, BLK, LANES), bf16),
            pltpu.VMEM((2, num_blocks, BLK, LANES), bf16),
            pltpu.VMEM((6, nz * ny, BLK, LANES), bf16),
            pltpu.VMEM((4, nz * ny, BLK, LANES), bf16),
            pltpu.VMEM((chips, BLK, LANES), bf16),
            pltpu.VMEM((chips, BLK, LANES), bf16),
            pltpu.VMEM((chips, BLK, LANES), jnp.float32),
            pltpu.VMEM(h_blocks.shape[1:], bf16),
            pltpu.VMEM(g_blocks.shape[1:], bf16),
            dma((2,)), dma((nz,)), dma((nz,)), dma((7,)), dma((3, nz)), dma((4,)), dma, dma((nz,)),
        ],
        compiler_params=pltpu.CompilerParams(collective_id=0, has_side_effects=True, vmem_limit_bytes=48 * 2**20),
        cost_estimate=pl.CostEstimate(flops=670_000_000, bytes_accessed=9 * 2**20, transcendentals=0),
    )(coeffs, h_blocks, h_cols, g_blocks, g_cols)


def solution(mesh, ny=NY):
    return jax.shard_map(
        functools.partial(per_device, ny),
        mesh=mesh,
        in_specs=(
            P("cls", None, "row", None),
            P("cls", None, None, None),
            P("cls", None, None),
            P("cls", None, None, None),
            P("cls", None, None),
        ),
        out_specs=P("cls", None, "row", None),
        check_vma=False,
    )
```

profile of v0, /device:TPU:1, one launch (start us, length us, event | category | flops | bytes accessed | tf_op | source)
XLA Modules:
  0.0 82.0 jit_solution(9042522701611597988)
XLA Ops:
  0.0 0.8 copy.6.hc
  0.8 0.8 copy.7.gc
  1.6 0.0 copy-start
  1.6 1.6 %copy-done = bf16[1,128,64,128]{3,2,1,0:T(8,128)(2,1)S(1)} copy-done((bf16[1,128,64,128]{3,2,1,0:T(8,128)(2,1)S(1)}, bf16[1,128,64,128]{3,2,1,0:T(8,128)(2,1)}, u32[]{:S(2)}) %copy-start) | copy-done | bytes 2097176
  3.2 0.0 copy-start.1
  3.2 1.2 %copy-done.1 = bf16[1,1,64,8192]{3,2,1,0:T(8,128)(2,1)S(1)} copy-done((bf16[1,1,64,8192]{3,2,1,0:T(8,128)(2,1)S(1)}, bf16[1,1,64,8192]{3,2,1,0:T(8,128)(2,1)}, u32[]{:S(2)}) %copy-start.1) | copy-done | bytes 1048600
  4.4 76.6 %shard_map.55 = bf16[1,1,64,8192]{3,2,1,0:T(8,128)(2,1)S(1)} custom-call(bf16[1,1,64,8192]{3,2,1,0:T(8,128)(2,1)S(1)} %copy-done.1, bf16[1,128,64,256]{3,2,1,0:T(8,128)(2,1)} %h_hbm.1, s32[1,128,4]{2,1,0:T(8,128)S(1)} %copy.6.hc, bf16[1,128,64,128]{3,2,1,0:T(8,128)(2,1)S(1)} %copy-done, s32[1,128,2]{2,1,0:T(8,128)S(1)} %copy.7.gc), custom_call_target="tpu_custom_call" | custom-call | flops 670000000 | bytes 9437184 | tf_op jit(solution)/shard_map/pallas_call | solution.py:231
  81.0 1.0 %copy.9 = bf16[1,1,64,8192]{3,2,1,0:T(8,128)(2,1)} copy(bf16[1,1,64,8192]{3,2,1,0:T(8,128)(2,1)S(1)} %shard_map.55) | data formatting | bytes 2097152
Async XLA Ops:
  1.6 1.6 %copy-start = (bf16[1,128,64,128]{3,2,1,0:T(8,128)(2,1)S(1)}, bf16[1,128,64,128]{3,2,1,0:T(8,128)(2,1)}, u32[]{:S(2)}) copy-start(bf16[1,128,64,128]{3,2,1,0:T(8,128)(2,1)} %g_hbm.1) | copy-start | bytes 6291460
  3.2 1.2 %copy-start.1 = (bf16[1,1,64,8192]{3,2,1,0:T(8,128)(2,1)S(1)}, bf16[1,1,64,8192]{3,2,1,0:T(8,128)(2,1)}, u32[]{:S(2)}) copy-start(bf16[1,1,64,8192]{3,2,1,0:T(8,128)(2,1)} %c_ref.1) | copy-start | bytes 3145732
where the time goes:
time: 82.2 us; the launch traced here: 82 us
  Pallas kernels  76.6 us (93%)
  local copies, waits for them, and re-layouts  5.35 us (7%)
    pallas_call x1, Pallas kernels, per_device(): pl.pallas_call(functools.partial(kernel, nz, ny), out_shape=jax.ShapeDtyp...  76.6 us
    unnamed x7, local copies, waits for them, and re-layouts  5.35 us

commit v1 on v0

--- a/solution.py
+++ b/solution.py
@@ -13,14 +13,15 @@
 LANES = 128
 KH = 4
 KG = 2
+DEPTH = 8
 
 
 def hop(k, nz):
     return lax.rem(((k + 1) // 2) * (2 * lax.rem(k, 2) - 1) + nz, nz)
 
 
-def kernel(nz, ny, c_ref, h_hbm, hc, g_hbm, gc, out_ref, slabs, halves, own, other, prod, back, beta, hv, gv,
-           load_sem, s1_send, s1_recv, x_send, x_recv, sib_recv, r_send, r_recv):
+def kernel(nz, ny, c_hbm, h_hbm, hc, g_hbm, gc, out_ref, rows, slabs, halves, own, other, prod, back, beta, hv, gv,
+           load_sem, enter_sem, s1_send, s1_recv, x_send, x_recv, sib_recv, r_send, r_recv):
     chips = nz * 2 * ny
     plane = 2 * ny
     cls, row = lax.axis_index("cls"), lax.axis_index("row")
@@ -35,20 +36,31 @@
     across = device(cls, z, 1 - xh, y, core)
     sibling = device(cls, z, xh, y, 1 - core)
 
-    h_copy = pltpu.make_async_copy(h_hbm.at[0], hv, load_sem.at[0])
-    g_copy = pltpu.make_async_copy(g_hbm.at[0], gv, load_sem.at[1])
+    c_copy = pltpu.make_async_copy(c_hbm.at[0, 0], rows, load_sem.at[0])
+    h_copy = pltpu.make_async_copy(h_hbm.at[0], hv, load_sem.at[1])
+    g_copy = pltpu.make_async_copy(g_hbm.at[0], gv, load_sem.at[2])
+    c_copy.start()
     h_copy.start()
     g_copy.start()
 
     barrier = pltpu.get_barrier_semaphore()
-
-    @pl.loop(1, chips)
+    along_y = [device(cls, z, xh, lax.rem(y + d, ny), core) for d in range(1, ny)]
+    along_z = [device(cls, lax.rem(z + d, nz), xh, y, core) for d in range(1, nz)]
+    for target in [pair, side, across, sibling] + along_y + along_z:
+        pl.semaphore_signal(barrier, inc=1, device_id=target, device_id_type=MESH)
+
+    c_copy.wait()
+
+    @pl.loop(0, nz * 2)
     def _(i):
-        pl.semaphore_signal(barrier, inc=1, device_id=(cls, lax.rem(p + i, chips) * 2 + core), device_id_type=MESH)
-
-    for target in (pair, side, sibling):
-        pl.semaphore_signal(barrier, inc=1, device_id=target, device_id_type=MESH)
-    pl.semaphore_wait(barrier, chips + 2)
+        for b in range(ny):
+            start = pl.multiple_of((i * ny + b) * LANES, LANES)
+            slabs[(i // 2) * plane + b * 2 + lax.rem(i, 2)] = rows[:, pl.ds(start, LANES)]
+
+    pl.semaphore_wait(barrier, ny + nz + 2)
+    for target in along_y:
+        pl.semaphore_signal(enter_sem, inc=1, device_id=target, device_id_type=MESH)
+    pl.semaphore_wait(enter_sem, ny - 1)
 
     def remote(src, dst, send, recv, target):
         return pltpu.make_async_remote_copy(
@@ -56,13 +68,8 @@
 
     mine = z * ny + y
 
-    @pl.loop(0, nz)
-    def _(k):
+    def scatter(k):
         to_z = lax.rem(z + hop(k, nz), nz)
-        for a in range(2):
-            for b in range(ny):
-                start = pl.multiple_of(((to_z * 2 + a) * ny + b) * LANES, LANES)
-                slabs[to_z * plane + b * 2 + a] = c_ref[0, 0, :, pl.ds(start, LANES)]
         for d in range(ny):
             to_y = lax.rem(y + d, ny)
             src = pl.ds(to_z * plane + to_y * 2, 2)
@@ -76,6 +83,10 @@
             else:
                 send()
 
+    @pl.loop(0, DEPTH)
+    def _(k):
+        scatter(k)
+
     own[core * 3 + xh, mine] = slabs[z * plane + y * 2]
     own[core * 3 + xh + 1, mine] = slabs[z * plane + y * 2 + 1]
 
@@ -83,7 +94,7 @@
 
     @pl.loop(0, chips)
     def _(t):
-        wide = c_ref[0, 0, :, pl.ds(pl.multiple_of(t * LANES, LANES), LANES)].astype(jnp.float32)
+        wide = rows[:, pl.ds(pl.multiple_of(t * LANES, LANES), LANES)].astype(jnp.float32)
         turned = pltpu.roll(wide, BLK, 1)
         zero = jnp.zeros_like(wide)
         halves[0, 2 * t] = jnp.where(low, wide, zero).astype(jnp.bfloat16)
@@ -96,7 +107,7 @@
     def beta_slab(q):
         tall = []
         for i in (2 * q, 2 * q + 1):
-            wide = [halves[0, hc[0, i, k]] + halves[1, hc[0, i, k + 1]] for k in range(0, KH, 2)]
+            wide = [halves[0, hc[0, k, i]] + halves[1, hc[0, k + 1, i]] for k in range(0, KH, 2)]
             tall.append(jnp.concatenate(wide, axis=1))
         blocks = hv[pl.ds(2 * q, 2)].reshape(2 * BLK, KH * BLK)
         both = lax.dot_general(jnp.concatenate(tall, axis=0), blocks, (((1,), (1,)), ((), ())),
@@ -132,6 +143,10 @@
         remote(transit, other.at[core * 2 + xh, zs], x_send.at[1], x_recv.at[1, k], side).start()
         remote(transit, straight, x_send.at[2], x_recv.at[2, k], across).start()
         remote(straight, straight, x_send.at[3], sib_recv.at[0], sibling).start()
+        @pl.when(k + DEPTH < nz)
+        def _():
+            scatter(k + DEPTH)
+
         for i in range(plane):
             beta_slab(k * plane + i)
 
@@ -160,8 +175,8 @@
 
     def alpha_block(q):
         i = 2 * q + core
-        x = jnp.concatenate([own_rows(hc[0, i, k]) for k in range(KH)], axis=0)
-        w = jnp.concatenate([other_rows(gc[0, i, k]) for k in range(KG)], axis=0)
+        x = jnp.concatenate([own_rows(hc[0, k, i]) for k in range(KH)], axis=0)
+        w = jnp.concatenate([other_rows(gc[0, k, i]) for k in range(KG)], axis=0)
         total = jnp.dot(hv[i], x, preferred_element_type=jnp.float32)
         total = total + jnp.dot(gv[i], w, preferred_element_type=jnp.float32)
         prod[q] = total.astype(jnp.bfloat16)
@@ -231,9 +246,10 @@
     return pl.pallas_call(
         functools.partial(kernel, nz, ny),
         out_shape=jax.ShapeDtypeStruct(coeffs.shape, bf16),
-        in_specs=[vmem, hbm, smem, hbm, smem],
+        in_specs=[hbm, hbm, smem, hbm, smem],
         out_specs=vmem,
         scratch_shapes=[
+            pltpu.VMEM(coeffs.shape[2:], bf16),
             pltpu.VMEM((chips, BLK, LANES), bf16),
             pltpu.VMEM((2, num_blocks, BLK, LANES), bf16),
             pltpu.VMEM((6, nz * ny, BLK, LANES), bf16),
@@ -243,11 +259,11 @@
             pltpu.VMEM((chips, BLK, LANES), jnp.float32),
             pltpu.VMEM(h_blocks.shape[1:], bf16),
             pltpu.VMEM(g_blocks.shape[1:], bf16),
-            dma((2,)), dma((nz,)), dma((nz,)), dma((7,)), dma((3, nz)), dma((4,)), dma, dma((nz,)),
+            dma((3,)), pltpu.SemaphoreType.REGULAR, dma((nz,)), dma((nz,)), dma((7,)), dma((3, nz)), dma((4,)), dma, dma((nz,)),
         ],
-        compiler_params=pltpu.CompilerParams(collective_id=0, has_side_effects=True, vmem_limit_bytes=48 * 2**20),
+        compiler_params=pltpu.CompilerParams(collective_id=0, has_side_effects=True, vmem_limit_bytes=62 * 2**20),
         cost_estimate=pl.CostEstimate(flops=670_000_000, bytes_accessed=9 * 2**20, transcendentals=0),
-    )(coeffs, h_blocks, h_cols, g_blocks, g_cols)
+    )(coeffs, h_blocks, jnp.swapaxes(h_cols, 1, 2), g_blocks, jnp.swapaxes(g_cols, 1, 2))
 
 
 def solution(mesh, ny=NY):

time: 82.2 us -> 76.5 us (0.931)
  local copies, waits for them, and re-layouts: 5.35 us -> 2.26 us
  Pallas kernels: 76.6 us -> 74.1 us
    unnamed x7 -> x1, local copies, waits for them, and re-layouts: 5.35 us -> 2.26 us
    pallas_call x1, Pallas kernels: 76.6 us -> 74.1 us  [per_device(): pl.pallas_call(functools.partial(kernel, nz, ny), out_shape=jax.ShapeDtyp...]
where the time goes in v1:
time: 76.5 us; the launch traced here: 76.4 us
  Pallas kernels  74.1 us (97%)
  local copies, waits for them, and re-layouts  2.26 us (3%)
    pallas_call x1, Pallas kernels, per_device(): pl.pallas_call(functools.partial(kernel, nz, ny), out_shape=jax.ShapeDtyp...  74.1 us
    unnamed x1, local copies, waits for them, and re-layouts  2.26 us

profile of v1, /device:TPU:1, one launch (start us, length us, event | category | flops | bytes accessed | tf_op | source)
XLA Modules:
  0.0 76.4 jit_solution(10298228639060139912)
XLA Ops:
  0.0 74.1 %shard_map.55 = bf16[1,1,64,8192]{3,2,1,0:T(8,128)(2,1)} custom-call(bf16[1,1,64,8192]{3,2,1,0:T(8,128)(2,1)} %c_hbm.1, bf16[1,128,64,256]{3,2,1,0:T(8,128)(2,1)} %h_hbm.1, s32[1,4,128]{2,1,0:T(4,128)} %bitcast.2, bf16[1,128,64,128]{3,2,1,0:T(8,128)(2,1)} %g_hbm.1, s32[1,2,128]{2,1,0:T(2,128)} %bitcast.3), custom_call_target="tpu_custom_call" | custom-call | flops 670000000 | bytes 9437184 | tf_op jit(solution)/shard_map/pallas_call | solution.py:246
  74.1 2.3 %copy.7 = bf16[1,1,64,8192]{3,2,1,0:T(8,128)(2,1)} copy(bf16[1,1,64,8192]{3,2,1,0:T(8,128)(2,1)} %shard_map.55) | data formatting | bytes 2097152

commit v2 on v1

--- a/solution.py
+++ b/solution.py
@@ -13,15 +13,16 @@
 LANES = 128
 KH = 4
 KG = 2
-DEPTH = 8
 
 
 def hop(k, nz):
+    if isinstance(k, int):
+        return ((k + 1) // 2 * (2 * (k % 2) - 1)) % nz
     return lax.rem(((k + 1) // 2) * (2 * lax.rem(k, 2) - 1) + nz, nz)
 
 
 def kernel(nz, ny, c_hbm, h_hbm, hc, g_hbm, gc, out_ref, rows, slabs, halves, own, other, prod, back, beta, hv, gv,
-           load_sem, enter_sem, s1_send, s1_recv, x_send, x_recv, sib_recv, r_send, r_recv):
+           load_sem, enter_sem, z_send, z_recv, x_send, x_recv, sib_recv, r_send, r_recv):
     chips = nz * 2 * ny
     plane = 2 * ny
     cls, row = lax.axis_index("cls"), lax.axis_index("row")
@@ -51,16 +52,17 @@
 
     c_copy.wait()
 
-    @pl.loop(0, nz * 2)
-    def _(i):
-        for b in range(ny):
-            start = pl.multiple_of((i * ny + b) * LANES, LANES)
-            slabs[(i // 2) * plane + b * 2 + lax.rem(i, 2)] = rows[:, pl.ds(start, LANES)]
-
+    def cut(half):
+        @pl.loop(0, nz)
+        def _(i):
+            for b in range(ny):
+                q = (i * 2 + half) * ny + b
+                slabs[q] = rows[:, pl.ds(pl.multiple_of(q * LANES, LANES), LANES)]
+
+    cut(1 - xh)
     pl.semaphore_wait(barrier, ny + nz + 2)
     for target in along_y:
         pl.semaphore_signal(enter_sem, inc=1, device_id=target, device_id_type=MESH)
-    pl.semaphore_wait(enter_sem, ny - 1)
 
     def remote(src, dst, send, recv, target):
         return pltpu.make_async_remote_copy(
@@ -68,32 +70,41 @@
 
     mine = z * ny + y
 
-    def scatter(k):
-        to_z = lax.rem(z + hop(k, nz), nz)
+    def slab(half, kind, k, d):
+        to_z, to_y = lax.rem(z + hop(k, nz), nz), lax.rem(y + d, ny)
+        row = core * 3 + (1 if kind == 0 else 2 * xh)
+        remote(slabs.at[(to_z * 2 + half) * ny + to_y], own.at[row, mine], z_send.at[kind], z_recv.at[kind, k],
+               device(cls, to_z, xh, to_y, core)).start()
+
+    for d in range(1, ny):
+        slab(1 - xh, 0, 0, d)
+
+    @pl.loop(1, nz)
+    def _(k):
+        slab(1 - xh, 0, k, 0)
+
+    pl.semaphore_wait(enter_sem, ny - 1)
+
+    for ks in [range(k, min(k + 2, nz)) for k in range(1, nz, 2)]:
+        for d in range(1, ny):
+            for k in ks:
+                slab(1 - xh, 0, k, d)
+
+    cut(xh)
+    for d in range(1, ny):
+        slab(xh, 1, 0, d)
+
+    for ks in [range(k, min(k + 2, nz)) for k in range(1, nz, 2)]:
         for d in range(ny):
-            to_y = lax.rem(y + d, ny)
-            src = pl.ds(to_z * plane + to_y * 2, 2)
-
-            def send():
-                remote(slabs.at[src], own.at[pl.ds(core * 3 + xh, 2), mine], s1_send.at[k], s1_recv.at[k],
-                       device(cls, to_z, xh, to_y, core)).start()
-
-            if d == 0:
-                pl.when(k > 0)(send)
-            else:
-                send()
-
-    @pl.loop(0, DEPTH)
-    def _(k):
-        scatter(k)
-
-    own[core * 3 + xh, mine] = slabs[z * plane + y * 2]
-    own[core * 3 + xh + 1, mine] = slabs[z * plane + y * 2 + 1]
+            for k in ks:
+                slab(xh, 1, k, d)
+
+    own[core * 3 + 1, mine] = slabs[(z * 2 + 1 - xh) * ny + y]
+    own[core * 3 + 2 * xh, mine] = slabs[(z * 2 + xh) * ny + y]
 
     low = lax.broadcasted_iota(jnp.int32, (BLK, LANES), 1) < BLK
 
-    @pl.loop(0, chips)
-    def _(t):
+    def halve(t):
         wide = rows[:, pl.ds(pl.multiple_of(t * LANES, LANES), LANES)].astype(jnp.float32)
         turned = pltpu.roll(wide, BLK, 1)
         zero = jnp.zeros_like(wide)
@@ -101,8 +112,6 @@
         halves[1, 2 * t + 1] = jnp.where(low, zero, wide).astype(jnp.bfloat16)
         halves[0, 2 * t + 1] = jnp.where(low, turned, zero).astype(jnp.bfloat16)
         halves[1, 2 * t] = jnp.where(low, zero, turned).astype(jnp.bfloat16)
-
-    h_copy.wait()
 
     def beta_slab(q):
         tall = []
@@ -117,44 +126,55 @@
     def group(k):
         return pl.ds(lax.rem(z - hop(k, nz) + nz, nz) * ny, ny)
 
-    def forward(k):
+    def arrived(kind, k):
+        row = core * 3 + (1 if kind == 0 else 2 * xh)
+
+        @pl.when(k == 0)
+        def _():
+            part = own.at[row, pl.ds(0, ny - 1)]
+            remote(part, part, z_send.at[kind], z_recv.at[kind, k], sibling).wait_recv()
+
+        @pl.when(k > 0)
+        def _():
+            part = own.at[row, group(k)]
+            remote(part, part, z_send.at[kind], z_recv.at[kind, k], sibling).wait_recv()
+
+    def forward(n, ref, k):
+        remote(ref, ref, x_send.at[n], x_recv.at[n, k], sibling).wait_recv()
+        remote(ref, ref, x_send.at[4 + n], sib_recv.at[1 + n], sibling).start()
+
+    def forward_pair(k):
+        forward(0, other.at[core * 2 + xh, group(k)], k)
+
+    @pl.loop(0, nz)
+    def _(k):
         zs = group(k)
-        arrived = (other.at[core * 2 + xh, zs], other.at[core * 2 + 1 - xh, zs], own.at[core * 3 + 2 * (1 - xh), zs])
-        for n, ref in enumerate(arrived):
-            remote(ref, ref, x_send.at[n], x_recv.at[n, k], sibling).wait_recv()
-            remote(ref, ref, x_send.at[4 + n], sib_recv.at[1 + n], sibling).start()
+        arrived(0, k)
+        transit = own.at[core * 3 + 1, zs]
+        remote(transit, other.at[core * 2 + xh, zs], x_send.at[1], x_recv.at[1, k], side).start()
+        remote(transit, own.at[core * 3 + 2 * xh, zs], x_send.at[2], x_recv.at[2, k], across).start()
+        for i in range(plane):
+            halve(k * plane + i)
+
+    h_copy.wait()
 
     @pl.loop(0, nz)
     def _(k):
         zs = group(k)
-
-        @pl.when(k == 0)
-        def _():
-            part = own.at[pl.ds(core * 3 + xh, 2), pl.ds(0, ny - 1)]
-            remote(part, part, s1_send.at[k], s1_recv.at[k], sibling).wait_recv()
-
-        @pl.when(k > 0)
-        def _():
-            part = own.at[pl.ds(core * 3 + xh, 2), zs]
-            remote(part, part, s1_send.at[k], s1_recv.at[k], sibling).wait_recv()
-
-        straight, transit = own.at[core * 3 + 2 * xh, zs], own.at[core * 3 + 1, zs]
+        arrived(1, k)
+        straight = own.at[core * 3 + 2 * xh, zs]
         remote(straight, other.at[core * 2 + xh, zs], x_send.at[0], x_recv.at[0, k], pair).start()
-        remote(transit, other.at[core * 2 + xh, zs], x_send.at[1], x_recv.at[1, k], side).start()
-        remote(transit, straight, x_send.at[2], x_recv.at[2, k], across).start()
         remote(straight, straight, x_send.at[3], sib_recv.at[0], sibling).start()
-        @pl.when(k + DEPTH < nz)
-        def _():
-            scatter(k + DEPTH)
-
+        forward(1, other.at[core * 2 + 1 - xh, zs], k)
+        forward(2, own.at[core * 3 + 2 * (1 - xh), zs], k)
         for i in range(plane):
             beta_slab(k * plane + i)
 
         @pl.when(k > 0)
         def _():
-            forward(k - 1)
-
-    forward(nz - 1)
+            forward_pair(k - 1)
+
+    forward_pair(nz - 1)
     g_copy.wait()
     theirs = (own.at[(1 - core) * 3 + 2 * xh], other.at[(1 - core) * 2 + xh], other.at[(1 - core) * 2 + 1 - xh],
               own.at[(1 - core) * 3 + 2 * (1 - xh)])
@@ -181,14 +201,13 @@
         total = total + jnp.dot(gv[i], w, preferred_element_type=jnp.float32)
         prod[q] = total.astype(jnp.bfloat16)
 
-    @pl.loop(0, nz)
-    def _(k):
-        n = nz - 1 - k
-        to_z = lax.rem(z + hop(n, nz), nz)
-        for i in range(plane):
-            alpha_block(to_z * plane + i)
-        for i in range(plane):
-            q = to_z * plane + i
+    @pl.loop(0, plane)
+    def _(i):
+        xy = lax.rem(p + i + 1, plane)
+        targets = [(n, lax.rem(z + hop(n, nz), nz) * plane + xy) for n in range(nz - 1, -1, -1)]
+        for _, q in targets:
+            alpha_block(q)
+        for n, q in targets:
 
             @pl.when(q != p)
             def _():
@@ -218,18 +237,9 @@
             total = beta[q] + back[q].astype(jnp.float32)
             out_ref[0, 0, :, pl.ds(pl.multiple_of(q * LANES, LANES), LANES)] = total.astype(jnp.bfloat16)
 
-    @pl.loop(0, nz)
-    def _(k):
-        @pl.when(k == 0)
-        def _():
-            part = slabs.at[pl.ds(0, 2 * (ny - 1))]
-            remote(part, part, s1_send.at[k], s1_recv.at[k], sibling).wait_send()
-
-        @pl.when(k > 0)
-        def _():
-            part = slabs.at[pl.ds(0, plane)]
-            remote(part, part, s1_send.at[k], s1_recv.at[k], sibling).wait_send()
-
+    for kind in range(2):
+        part = slabs.at[pl.ds(0, nz * ny - 1)]
+        remote(part, part, z_send.at[kind], z_recv.at[kind, 0], sibling).wait_send()
     for n in range(7):
         remote(own.at[0], own.at[0], x_send.at[n], sib_recv.at[0], sibling).wait_send()
     part = prod.at[pl.ds(0, chips - 1)]
@@ -242,7 +252,7 @@
     nz = chips // (2 * ny)
     bf16, dma = jnp.bfloat16, pltpu.SemaphoreType.DMA
     vmem, smem = pl.BlockSpec(memory_space=pltpu.VMEM), pl.BlockSpec(memory_space=pltpu.SMEM)
-    hbm = pl.BlockSpec(memory_space=pl.ANY)
+    hbm = pl.BlockSpec(memory_space=pltpu.HBM)
     return pl.pallas_call(
         functools.partial(kernel, nz, ny),
         out_shape=jax.ShapeDtypeStruct(coeffs.shape, bf16),
@@ -259,9 +269,9 @@
             pltpu.VMEM((chips, BLK, LANES), jnp.float32),
             pltpu.VMEM(h_blocks.shape[1:], bf16),
             pltpu.VMEM(g_blocks.shape[1:], bf16),
-            dma((3,)), pltpu.SemaphoreType.REGULAR, dma((nz,)), dma((nz,)), dma((7,)), dma((3, nz)), dma((4,)), dma, dma((nz,)),
+            dma((3,)), pltpu.SemaphoreType.REGULAR, dma((2,)), dma((2, nz)), dma((7,)), dma((3, nz)), dma((4,)), dma, dma((nz,)),
         ],
-        compiler_params=pltpu.CompilerParams(collective_id=0, has_side_effects=True, vmem_limit_bytes=62 * 2**20),
+        compiler_params=pltpu.CompilerParams(collective_id=0, has_side_effects=True, vmem_limit_bytes=52 * 2**20),
         cost_estimate=pl.CostEstimate(flops=670_000_000, bytes_accessed=9 * 2**20, transcendentals=0),
     )(coeffs, h_blocks, jnp.swapaxes(h_cols, 1, 2), g_blocks, jnp.swapaxes(g_cols, 1, 2))
 

time: 76.5 us -> 72.9 us (0.953)
  Pallas kernels: 74.1 us -> 70.5 us
    pallas_call x1, Pallas kernels: 74.1 us -> 70.5 us  [per_device(): pl.pallas_call(functools.partial(kernel, nz, ny), out_shape=jax.ShapeDtyp...]
    unnamed x1 -> x5, local copies, waits for them, and re-layouts: 2.26 us -> 2.33 us
where the time goes in v2:
time: 72.9 us; the launch traced here: 72.8 us
  Pallas kernels  70.5 us (97%)
  local copies, waits for them, and re-layouts  2.33 us (3%)
    pallas_call x1, Pallas kernels, per_device(): pl.pallas_call(functools.partial(kernel, nz, ny), out_shape=jax.ShapeDtyp...  70.5 us
    unnamed x5, local copies, waits for them, and re-layouts  2.33 us

profile of v2, /device:TPU:1, one launch (start us, length us, event | category | flops | bytes accessed | tf_op | source)
XLA Modules:
  0.0 72.8 jit_solution(1940672798814040670)
XLA Ops:
  0.0 0.0 copy-start
  0.0 0.7 copy-done
  0.7 0.0 copy-start.1
  0.7 0.7 copy-done.1
  1.4 70.5 %shard_map.55 = bf16[1,1,64,8192]{3,2,1,0:T(8,128)(2,1)S(1)} custom-call(bf16[1,1,64,8192]{3,2,1,0:T(8,128)(2,1)} %c_hbm.1, bf16[1,128,64,256]{3,2,1,0:T(8,128)(2,1)} %h_hbm.1, s32[1,4,128]{2,1,0:T(4,128)S(1)} %bitcast.2, bf16[1,128,64,128]{3,2,1,0:T(8,128)(2,1)} %g_hbm.1, s32[1,2,128]{2,1,0:T(2,128)S(1)} %bitcast.3), custom_call_target="tpu_custom_call" | custom-call | flops 670000000 | bytes 9437184 | tf_op jit(solution)/shard_map/pallas_call | solution.py:256
  71.8 1.0 %copy.7 = bf16[1,1,64,8192]{3,2,1,0:T(8,128)(2,1)} copy(bf16[1,1,64,8192]{3,2,1,0:T(8,128)(2,1)S(1)} %shard_map.55) | data formatting | bytes 2097152
Async XLA Ops:
  0.0 0.7 copy-start
  0.7 0.7 copy-start.1

commit v3 on v2

--- a/solution.py
+++ b/solution.py
@@ -143,9 +143,6 @@
         remote(ref, ref, x_send.at[n], x_recv.at[n, k], sibling).wait_recv()
         remote(ref, ref, x_send.at[4 + n], sib_recv.at[1 + n], sibling).start()
 
-    def forward_pair(k):
-        forward(0, other.at[core * 2 + xh, group(k)], k)
-
     @pl.loop(0, nz)
     def _(k):
         zs = group(k)
@@ -165,16 +162,18 @@
         straight = own.at[core * 3 + 2 * xh, zs]
         remote(straight, other.at[core * 2 + xh, zs], x_send.at[0], x_recv.at[0, k], pair).start()
         remote(straight, straight, x_send.at[3], sib_recv.at[0], sibling).start()
-        forward(1, other.at[core * 2 + 1 - xh, zs], k)
-        forward(2, own.at[core * 3 + 2 * (1 - xh), zs], k)
         for i in range(plane):
             beta_slab(k * plane + i)
 
-        @pl.when(k > 0)
-        def _():
-            forward_pair(k - 1)
-
-    forward_pair(nz - 1)
+    @pl.loop(0, nz)
+    def _(k):
+        forward(1, other.at[core * 2 + 1 - xh, group(k)], k)
+        forward(2, own.at[core * 3 + 2 * (1 - xh), group(k)], k)
+
+    @pl.loop(0, nz)
+    def _(k):
+        forward(0, other.at[core * 2 + xh, group(k)], k)
+
     g_copy.wait()
     theirs = (own.at[(1 - core) * 3 + 2 * xh], other.at[(1 - core) * 2 + xh], other.at[(1 - core) * 2 + 1 - xh],
               own.at[(1 - core) * 3 + 2 * (1 - xh)])

time: 72.9 us -> 70.8 us (0.971)
  Pallas kernels: 70.5 us -> 68.3 us
    pallas_call x1, Pallas kernels: 70.5 us -> 68.3 us  [per_device(): pl.pallas_call(functools.partial(kernel, nz, ny), out_shape=jax.ShapeDtyp...]
where the time goes in v3:
time: 70.8 us; the launch traced here: 70.7 us
  Pallas kernels  68.3 us (96%)
  local copies, waits for them, and re-layouts  2.33 us (3%)
    pallas_call x1, Pallas kernels, per_device(): pl.pallas_call(functools.partial(kernel, nz, ny), out_shape=jax.ShapeDtyp...  68.3 us
    unnamed x5, local copies, waits for them, and re-layouts  2.33 us

profile of v3, /device:TPU:1, one launch (start us, length us, event | category | flops | bytes accessed | tf_op | source)
XLA Modules:
  0.0 70.7 jit_solution(8497073617571683049)
XLA Ops:
  0.0 0.0 copy-start
  0.0 0.7 copy-done
  0.7 0.0 copy-start.1
  0.7 0.7 copy-done.1
  1.4 68.3 %shard_map.55 = bf16[1,1,64,8192]{3,2,1,0:T(8,128)(2,1)S(1)} custom-call(bf16[1,1,64,8192]{3,2,1,0:T(8,128)(2,1)} %c_hbm.1, bf16[1,128,64,256]{3,2,1,0:T(8,128)(2,1)} %h_hbm.1, s32[1,4,128]{2,1,0:T(4,128)S(1)} %bitcast.2, bf16[1,128,64,128]{3,2,1,0:T(8,128)(2,1)} %g_hbm.1, s32[1,2,128]{2,1,0:T(2,128)S(1)} %bitcast.3), custom_call_target="tpu_custom_call" | custom-call | flops 670000000 | bytes 9437184 | tf_op jit(solution)/shard_map/pallas_call | solution.py:255
  69.7 1.0 %copy.7 = bf16[1,1,64,8192]{3,2,1,0:T(8,128)(2,1)} copy(bf16[1,1,64,8192]{3,2,1,0:T(8,128)(2,1)S(1)} %shard_map.55) | data formatting | bytes 2097152
Async XLA Ops:
  0.0 0.7 copy-start
  0.7 0.7 copy-start.1

commit v4 on v3

--- a/solution.py
+++ b/solution.py
@@ -69,6 +69,7 @@
             src_ref=src, dst_ref=dst, send_sem=send, recv_sem=recv, device_id=target, device_id_type=MESH)
 
     mine = z * ny + y
+    far_y = sorted(range(1, ny), key=lambda d: -min(d, ny - d))
 
     def slab(half, kind, k, d):
         to_z, to_y = lax.rem(z + hop(k, nz), nz), lax.rem(y + d, ny)
@@ -86,7 +87,7 @@
     pl.semaphore_wait(enter_sem, ny - 1)
 
     for ks in [range(k, min(k + 2, nz)) for k in range(1, nz, 2)]:
-        for d in range(1, ny):
+        for d in far_y:
             for k in ks:
                 slab(1 - xh, 0, k, d)
 
@@ -95,7 +96,7 @@
         slab(xh, 1, 0, d)
 
     for ks in [range(k, min(k + 2, nz)) for k in range(1, nz, 2)]:
-        for d in range(ny):
+        for d in far_y + [0]:
             for k in ks:
                 slab(xh, 1, k, d)
 
@@ -204,17 +205,18 @@
     def _(i):
         xy = lax.rem(p + i + 1, plane)
         targets = [(n, lax.rem(z + hop(n, nz), nz) * plane + xy) for n in range(nz - 1, -1, -1)]
-        for _, q in targets:
-            alpha_block(q)
-        for n, q in targets:
-
-            @pl.when(q != p)
-            def _():
-                remote(prod.at[q], back.at[p], r_send, r_recv.at[n], (cls, 2 * q + core)).start()
-
-            @pl.when(q == p)
-            def _():
-                back[p] = prod[p]
+        for part in (targets[: nz // 2], targets[nz // 2 :]):
+            for _, q in part:
+                alpha_block(q)
+            for n, q in part:
+
+                @pl.when(q != p)
+                def _():
+                    remote(prod.at[q], back.at[p], r_send, r_recv.at[n], (cls, 2 * q + core)).start()
+
+                @pl.when(q == p)
+                def _():
+                    back[p] = prod[p]
 
     @pl.loop(0, nz)
     def _(k):

time: 70.8 us -> 70 us (0.989)
  Pallas kernels: 68.3 us -> 67.5 us
    pallas_call x1, Pallas kernels: 68.3 us -> 67.5 us  [per_device(): pl.pallas_call(functools.partial(kernel, nz, ny), out_shape=jax.ShapeDtyp...]
where the time goes in v4:
time: 70 us; the launch traced here: 69.9 us
  Pallas kernels  67.5 us (96%)
  local copies, waits for them, and re-layouts  2.33 us (3%)
    pallas_call x1, Pallas kernels, per_device(): pl.pallas_call(functools.partial(kernel, nz, ny), out_shape=jax.ShapeDtyp...  67.5 us
    unnamed x5, local copies, waits for them, and re-layouts  2.33 us

profile of v4, /device:TPU:1, one launch (start us, length us, event | category | flops | bytes accessed | tf_op | source)
XLA Modules:
  0.0 69.9 jit_solution(11987834752770625541)
XLA Ops:
  0.0 0.0 copy-start
  0.0 0.7 copy-done
  0.7 0.0 copy-start.1
  0.7 0.7 copy-done.1
  1.4 67.5 %shard_map.55 = bf16[1,1,64,8192]{3,2,1,0:T(8,128)(2,1)S(1)} custom-call(bf16[1,1,64,8192]{3,2,1,0:T(8,128)(2,1)} %c_hbm.1, bf16[1,128,64,256]{3,2,1,0:T(8,128)(2,1)} %h_hbm.1, s32[1,4,128]{2,1,0:T(4,128)S(1)} %bitcast.2, bf16[1,128,64,128]{3,2,1,0:T(8,128)(2,1)} %g_hbm.1, s32[1,2,128]{2,1,0:T(2,128)S(1)} %bitcast.3), custom_call_target="tpu_custom_call" | custom-call | flops 670000000 | bytes 9437184 | tf_op jit(solution)/shard_map/pallas_call | solution.py:257
  68.9 1.0 %copy.7 = bf16[1,1,64,8192]{3,2,1,0:T(8,128)(2,1)} copy(bf16[1,1,64,8192]{3,2,1,0:T(8,128)(2,1)S(1)} %shard_map.55) | data formatting | bytes 2097152
Async XLA Ops:
  0.0 0.7 copy-start
  0.7 0.7 copy-start.1
